TPU v7x, 32 devices: a whole 2x2x4 slice. The times are simulated.
32 devices in a mesh: layer: 1, dp: 32 (over z, y, x, core).
Axes of the slice: x: 2, y: 2, z: 4, core: 2. Of those that a mesh axis runs over, the one named last changes fastest.
Arguments:
- activations: bfloat16 [1, 4096, 5120], P('layer', 'dp'), may hold values from -6 to 6
- out_grads: bfloat16 [1, 4096, 5120], P('layer', 'dp'), may hold values from -6 to 6
- projectors: bfloat16 [1, 5120, 128], P('layer'), may hold values from -0.078125 to 0.078125
- rewards: float32 [128], P('dp'), may hold values from -8 to 8
- lengths: int32 [128], P('dp'), may hold values from 1 to 32, 3072 in all
- pairing: int32 [64, 2], P('dp'), may hold values from 0 to 3, as said below
- queries: bfloat16 [1, 256, 4096], P('layer', 'dp'), may hold values from -0.0078125 to 0.0078125
Outputs:
- scores: float32 [64, 256], P('dp', 'layer')
Inputs may be any that keep to these rules, and one draw needn't show every extreme that they name: `pairing`: the 2 pairs of one dp index name each of that index's 2 * 2 sequences exactly once.
All inputs are finite; a program needn't handle non-finite values. No bound on the sum of `lengths` on one device may be relied on, other than what follows from the above.
Results may differ from a plain program's by a relative error of at most 0.0029.
Values may be sent and summed in bfloat16 or wider, within the bound.
A program may use at most 64 MiB of HBM per device.

v0:
```python
import jax
import jax.numpy as jnp
from jax import lax
from jax.sharding import PartitionSpec as P


def local(activations, out_grads, projectors, rewards, lengths, pairing, queries):
    half = projectors.shape[2] // 2
    seq_count = lengths.shape[0]
    seq_len = activations.shape[1] // seq_count
    proj_act = jnp.dot(activations[0], projectors[0, :, :half], preferred_element_type=jnp.float32)
    proj_grad = jnp.dot(out_grads[0], projectors[0, :, half:], preferred_element_type=jnp.float32)
    places = jnp.arange(seq_len, dtype=jnp.int32)
    live_mask = (places[None, :] < lengths[:, None]).astype(jnp.float32)
    grad_seq = proj_grad.reshape(seq_count, seq_len, half) * live_mask[:, :, None]
    act_seq = proj_act.reshape(seq_count, seq_len, half)
    seq_grads = jnp.einsum(
        "stk,stj->skj", grad_seq, act_seq, precision=lax.Precision.HIGHEST
    ).reshape(seq_count, half * half)
    chosen = pairing[:, 0]
    rejected = pairing[:, 1]
    margin_weight = 1.0 - jax.nn.sigmoid(rewards[chosen] - rewards[rejected])
    train_grads = (margin_weight[:, None] * (seq_grads[rejected] - seq_grads[chosen])).astype(
        jnp.bfloat16
    )
    partial_scores = jnp.dot(
        train_grads,
        lax.all_gather(queries, "dp", axis=1, tiled=True)[0].T,
        preferred_element_type=jnp.float32,
    )
    return lax.psum_scatter(partial_scores, "layer", scatter_dimension=1, tiled=True)


def solution(mesh):
    return jax.shard_map(
        local,
        mesh=mesh,
        in_specs=(
            P("layer", "dp", None),
            P("layer", "dp", None),
            P("layer", None, None),
            P("dp"),
            P("dp"),
            P("dp", None),
            P("layer", "dp", None),
        ),
        out_specs=P("dp", "layer"),
        check_vma=False,
    )
```

profile of v0, /device:TPU:0, one launch (start us, length us, event | category | flops | bytes accessed | tf_op | source)
XLA Modules:
  0.0 79.0 jit_solution(12991138880171914014)
XLA Ops:
  6.5 0.0 copy-start
  6.5 0.0 all-gather.2.cloned.1.call-start
  6.5 0.7 all-gather.2.cloned.1.call-update
  7.3 1.0 %fusion.12 = (s32[2]{0:T(128)S(1)}, s32[2]{0:T(128)S(1)}) fusion(s32[2,2]{1,0:T(2,128)} %param.12), kind=kLoop, calls=%fused_computation.20 | loop fusion | flops 12 | bytes 32 | tf_op jit(solution)/shard_map/select_n | solution.py:22
  8.2 1.3 %gather_fusion = f32[2]{0:T(128)S(1)} fusion(f32[4]{0:T(128)} %param.10, s32[1024]{0:T(1024)S(1)} %get-tuple-element.8), kind=kCustom, calls=%fused_computation | custom fusion | bytes 24 | tf_op jit(solution)/shard_map/gather | solution.py:22
  9.5 1.3 %gather_fusion.1 = f32[2]{0:T(128)S(1)} fusion(f32[4]{0:T(128)} %param.10, s32[1024]{0:T(1024)S(1)} %get-tuple-element.7), kind=kCustom, calls=%fused_computation.1 | custom fusion | bytes 24 | tf_op jit(solution)/shard_map/gather | solution.py:22
  10.8 0.7 fusion.11
  11.6 0.0 copy-done
  11.6 0.0 copy-start.1
  11.6 0.0 copy-start.2
  11.6 2.0 %fusion.2 = f32[4,32,64]{2,1,0:T(8,128)S(1)} fusion(bf16[4,32,5120]{2,1,0:T(8,128)(2,1)S(1)} %bitcast.19, bf16[1,5120,128]{2,1,0:T(8,128)(2,1)} %param.9), kind=kOutput, calls=%fused_computation.6 | convolution fusion | flops 83886080 | bytes 2654208 | tf_op jit(solution)/shard_map/dot_general | solution.py:11
  13.5 0.0 copy-done.1
  13.5 0.1 copy-done.2
  13.7 0.7 fusion.8
  14.4 0.4 fusion.14
  14.8 0.1 reshape.41
  14.9 0.6 gather_fusion.3
  15.5 0.6 gather_fusion.2
  16.1 53.3 %all-gather.2.cloned.1.call-done = bf16[1,256,4096]{2,1,0:T(8,128)(2,1)} async-done(((bf16[1,8,4096]{2,1,0:T(8,128)(2,1)}), bf16[1,256,4096]{2,1,0:T(8,128)(2,1)}) %all-gather.2.cloned.1.call-update) | async-done | bytes 2097168 | tf_op jit(solution)/shard_map/all_gather | solution.py:28
  69.3 2.8 %fusion = f32[2,256]{1,0:T(2,128)} fusion(bf16[1,256,4096]{2,1,0:T(8,128)(2,1)} %all-gather.2.cloned.1.call-done, f32[2,4096]{1,0:T(2,128)S(1)} %gather_fusion.2, f32[2,4096]{1,0:T(2,128)S(1)} %gather_fusion.3, f32[2]{0:T(128)S(1)} %divide_subtract_fusion), kind=kOutput, calls=%fused_computation.4 | convolution fusion | flops 4218880 | bytes 2164744 | tf_op jit(solution)/shard_map/dot_general | solution.py:26
  (2 shorter events, 0.0 us)
Async XLA Ops:
  6.5 5.0 %copy-start = (bf16[1,128,5120]{2,1,0:T(8,128)(2,1)S(1)}, bf16[1,128,5120]{2,1,0:T(8,128)(2,1)}, u32[]{:S(2)}) copy-start(bf16[1,128,5120]{2,1,0:T(8,128)(2,1)} %param.7) | copy-start | bytes 3932164
  6.5 62.8 %all-gather.2.cloned.1.call-start = ((), (), s32[]{:S(2)}) async-start(), calls=%async_computation | async-start | bytes 2162688 | tf_op jit(solution)/shard_map/all_gather | solution.py:28
  11.6 2.0 %copy-start.1 = (bf16[1,128,5120]{2,1,0:T(8,128)(2,1)S(1)}, bf16[1,128,5120]{2,1,0:T(8,128)(2,1)}, u32[]{:S(2)}) copy-start(bf16[1,128,5120]{2,1,0:T(8,128)(2,1)} %param.8) | copy-start | bytes 3932164
  11.6 2.1 %copy-start.2 = (bf16[1,5120,128]{2,1,0:T(8,128)(2,1)S(1)}, bf16[1,5120,128]{2,1,0:T(8,128)(2,1)}, u32[]{:S(2)}) copy-start(bf16[1,5120,128]{2,1,0:T(8,128)(2,1)} %param.9) | copy-start | bytes 3932164
Sparse Core Ops, SparseCore 0:
  10.2 59.0 all-gather.1
where the time goes:
time: 79.2 us; the launch traced here: 79 us
  waiting for transfers between devices  54 us (68%)
  between operations  13.4 us (17%)
  matrix products  5.89 us (7%)
  local copies, waits for them, and re-layouts  3.98 us (5%)
  other arithmetic  1.71 us (2%)
    all_gather x1, waiting for transfers between devices, local(): lax.all_gather(queries, 'dp', axis=1, tiled=True)[0]  53.3 us
    dot_general x1, matrix products, local(): jnp.dot(train_grads, lax.all_gather(queries, 'dp', axis=1, tiled=True)[0]...  2.82 us
    gather x2, local copies, waits for them, and re-layouts, local(): margin_weight = 1.0 - jax.nn.sigmoid(rewards[chosen] - rewards[rejected])  2.59 us
    dot_general x1, matrix products, local(): jnp.dot(activations[0], projectors[0, :, :half], preferred_element_type=j...  1.96 us
  transfers between devices with their start and end apart: 1, of which 1 were waited for; matrix products, arithmetic and copies ran while one was open for 11% of the time, Pallas kernels for 0%

commit v1 on v0

v1 whole, which is shorter than its diff:
```python
import functools
import math

import jax
import jax.numpy as jnp
from jax import lax
from jax.experimental import pallas as pl
from jax.experimental.pallas import tpu as pltpu
from jax.sharding import PartitionSpec as P

LANES = 128
CHUNKS = 4


def kernel(
    outer, reps, inner,
    act_ref, grad_ref, proj_ref, rewards_ref, lengths_ref, pairing_ref, queries_ref, out_ref,
    tokens, weights, query_all, outer_products, train_send, train_recv, part_send, part_recv,
    load_sem, own_sem, q1_send, q1_recv, q2_send, q2_recv, t_send, t_recv, p_send, p_recv,
):
    group = outer * inner
    me = lax.axis_index("dp")
    place = me % inner
    rep = (me // inner) % reps
    slab = me // (inner * reps)
    mine = slab * inner + place
    slots, width = act_ref.shape[1], act_ref.shape[2]
    seq_count = lengths_ref.shape[0]
    seq_len = slots // seq_count
    half = proj_ref.shape[2] // 2
    pair_count = pairing_ref.shape[0]
    entries = queries_ref.shape[2] // group
    rows = entries // LANES

    def member(step):
        other = (mine + step) % group
        return other, (other // inner * reps + rep) * inner + other % inner

    def twin(step):
        return (slab * reps + (rep + step) % reps) * inner + place

    part = width // CHUNKS
    loads = []
    for c in range(CHUNKS):
        cols = pl.ds(c * part, part)
        loads.append([
            pltpu.make_async_copy(proj_ref.at[0, cols, :], weights.at[cols, :], load_sem.at[c, 0]),
            pltpu.make_async_copy(
                act_ref.at[0, :, cols], tokens.at[pl.ds(0, slots), cols], load_sem.at[c, 1]
            ),
            pltpu.make_async_copy(
                grad_ref.at[0, :, cols], tokens.at[pl.ds(slots, slots), cols], load_sem.at[c, 2]
            ),
        ])
        for copy in loads[-1]:
            copy.start()

    def chunk_of(index):
        return queries_ref.at[0, :, pl.ds(pl.multiple_of(index * entries, LANES), entries)]

    own = pltpu.make_async_copy(chunk_of(mine), query_all.at[slab, rep, place], own_sem)
    own.start()

    barrier = pltpu.get_barrier_semaphore()
    for step in range(1, group):
        pl.semaphore_signal(
            barrier, inc=1, device_id={"dp": member(step)[1]}, device_id_type=pl.DeviceIdType.MESH
        )
    for step in range(1, reps):
        pl.semaphore_signal(
            barrier, inc=1, device_id={"dp": twin(step)}, device_id_type=pl.DeviceIdType.MESH
        )
    pl.semaphore_wait(barrier, group - 1 + reps - 1)

    def send(src, dst, send_sem, recv_sem, device):
        copy = pltpu.make_async_remote_copy(
            src_ref=src, dst_ref=dst, send_sem=send_sem, recv_sem=recv_sem,
            device_id={"dp": device}, device_id_type=pl.DeviceIdType.MESH,
        )
        copy.start()
        return copy

    first = []
    for step in range(1, group):
        other, device = member(step)
        first.append(send(
            chunk_of(other), query_all.at[slab, rep, place], q1_send.at[step], q1_recv.at[step], device
        ))

    lane = lax.broadcasted_iota(jnp.int32, (seq_len, LANES), 1)
    spot = lax.broadcasted_iota(jnp.int32, (seq_len, LANES), 0)
    signs = []
    for s in range(seq_count):
        sign = []
        for i in range(pair_count):
            is_chosen = (pairing_ref[i, 0] == s).astype(jnp.float32)
            is_rejected = (pairing_ref[i, 1] == s).astype(jnp.float32)
            sign.append(is_rejected - is_chosen)
        both = jnp.where(lane < half, sign[0], sign[1])
        signs.append(jnp.where(spot < lengths_ref[s], both, 0.0))
    signs = jnp.concatenate(signs, axis=0)
    pair_weights = []
    for i in range(pair_count):
        margin = jnp.float32(0.0)
        for s in range(seq_count):
            reward = rewards_ref[s]
            margin = margin + jnp.where(pairing_ref[i, 0] == s, reward, 0.0)
            margin = margin - jnp.where(pairing_ref[i, 1] == s, reward, 0.0)
        pair_weights.append(1.0 - jax.nn.sigmoid(jnp.full((half, LANES), margin, jnp.float32)))

    projected = jnp.zeros((2 * slots, 2 * half), jnp.float32)
    for c in range(CHUNKS):
        for copy in loads[c]:
            copy.wait()
        cols = pl.ds(c * part, part)
        projected += jnp.dot(tokens[:, cols], weights[cols, :], preferred_element_type=jnp.float32)

    own.wait()
    for copy in first:
        copy.wait()
    second = [
        send(
            query_all.at[:, rep], query_all.at[:, rep], q2_send.at[step], q2_recv.at[step], twin(step)
        )
        for step in range(1, reps)
    ]

    token_lane = lax.broadcasted_iota(jnp.int32, (slots, LANES), 1)
    act = projected[:slots]
    act = jnp.where(token_lane < half, act, pltpu.roll(act, half, 1))
    grad = projected[slots:]
    grad = jnp.where(token_lane < half, pltpu.roll(grad, half, 1), grad)
    products = lax.dot_general(
        grad * signs, act, (((0,), (0,)), ((), ())),
        precision=lax.Precision.HIGHEST, preferred_element_type=jnp.float32,
    )
    outer_products[...] = products * jnp.concatenate(pair_weights, axis=0)
    lines = pair_count * half // 2
    even = outer_products[pl.ds(0, lines, stride=2), :]
    odd = outer_products[pl.ds(1, lines, stride=2), :]
    flat_lane = lax.broadcasted_iota(jnp.int32, (lines, LANES), 1)
    flat = jnp.where(flat_lane < half, even, odd)
    for g in range(group):
        for i in range(pair_count):
            start = i * (half // 2) + g * rows
            train_send[g, i * rows:(i + 1) * rows, :] = flat[start:start + rows]
    train_recv[mine] = train_send[mine]
    train_copies = []
    for step in range(1, group):
        other, device = member(step)
        train_copies.append(send(
            train_send.at[other], train_recv.at[mine], t_send.at[step], t_recv.at[step], device
        ))

    for copy in second:
        copy.wait()
    query_rows = query_all[...].astype(jnp.float32).reshape(-1, entries).astype(jnp.bfloat16)
    for copy in train_copies:
        copy.wait()

    received = train_recv[...].reshape(group * pair_count, rows, LANES)
    left = jnp.concatenate([received[:, r, :] for r in range(rows)], axis=1).astype(jnp.bfloat16)
    partial = lax.dot_general(
        left, query_rows, (((1,), (1,)), ((), ())), preferred_element_type=jnp.float32
    )
    for g in range(group):
        part_send[g] = partial[g * pair_count:(g + 1) * pair_count]
    part_recv[mine] = part_send[mine]
    part_copies = []
    for step in range(1, group):
        other, device = member(step)
        part_copies.append(send(
            part_send.at[other], part_recv.at[mine], p_send.at[step], p_recv.at[step], device
        ))
    for copy in part_copies:
        copy.wait()
    total = part_recv[0]
    for g in range(1, group):
        total += part_recv[g]
    out_ref[...] = total


def solution(mesh):
    devices = mesh.shape["dp"]
    inner = math.gcd(devices, 2)
    outer = math.gcd(devices // inner, 4)
    reps = devices // (inner * outer)
    group = outer * inner

    def local(activations, out_grads, projectors, rewards, lengths, pairing, queries):
        slots, width = activations.shape[1:]
        half = projectors.shape[2] // 2
        pair_count = pairing.shape[0]
        per_device, length = queries.shape[1:]
        entries = length // group
        rows = pair_count * entries // LANES
        dma = lambda *shape: pltpu.SemaphoreType.DMA(shape)
        smem = pl.BlockSpec(memory_space=pltpu.SMEM)
        hbm = pl.BlockSpec(memory_space=pl.ANY)
        partial_scores = pl.pallas_call(
            functools.partial(kernel, outer, reps, inner),
            out_shape=jax.ShapeDtypeStruct((pair_count, devices * per_device), jnp.float32),
            in_specs=[hbm, hbm, hbm, smem, smem, smem, hbm],
            out_specs=pl.BlockSpec(memory_space=pltpu.VMEM),
            scratch_shapes=[
                pltpu.VMEM((2 * slots, width), jnp.bfloat16),
                pltpu.VMEM((width, 2 * half), jnp.bfloat16),
                pltpu.VMEM((outer, reps, inner, per_device, entries), jnp.bfloat16),
                pltpu.VMEM((pair_count * half, LANES), jnp.float32),
                pltpu.VMEM((group, rows, LANES), jnp.float32),
                pltpu.VMEM((group, rows, LANES), jnp.float32),
                pltpu.VMEM((group, pair_count, devices * per_device), jnp.float32),
                pltpu.VMEM((group, pair_count, devices * per_device), jnp.float32),
                dma(CHUNKS, 3), dma(), dma(group), dma(group), dma(reps), dma(reps),
                dma(group), dma(group), dma(group), dma(group),
            ],
            compiler_params=pltpu.CompilerParams(
                collective_id=0, has_side_effects=True, vmem_limit_bytes=40 * 1024 * 1024
            ),
        )(activations, out_grads, projectors, rewards, lengths, pairing, queries)
        return lax.psum_scatter(partial_scores, "layer", scatter_dimension=1, tiled=True)

    return jax.shard_map(
        local,
        mesh=mesh,
        in_specs=(
            P("layer", "dp", None),
            P("layer", "dp", None),
            P("layer", None, None),
            P("dp"),
            P("dp"),
            P("dp", None),
            P("layer", "dp", None),
        ),
        out_specs=P("dp", "layer"),
        check_vma=False,
    )
```

time: 79.2 us -> 27.7 us (0.35)
  waiting for transfers between devices: 54 us -> 0 us
  Pallas kernels: 0 us -> 20 us
  between operations: 13.4 us -> 0.02 us
  matrix products: 5.89 us -> 0 us
  local copies, waits for them, and re-layouts: 3.98 us -> 7.35 us
  other arithmetic: 1.71 us -> 0 us
    all_gather x1 -> x0, waiting for transfers between devices: 53.3 us -> none  [local(): lax.all_gather(queries, 'dp', axis=1, tiled=True)[0]]
    pallas_call x0 -> x1, Pallas kernels: none -> 20 us  [local(): pl.pallas_call(functools.partial(kernel, outer, reps, inner), out_shape=j...]
    unnamed x6 -> x15, local copies, waits for them, and re-layouts: 0.14 us -> 7.35 us
    dot_general x4 -> x0, matrix products: 5.89 us -> none  [the longest x1 2.82 us: local(): jnp.dot(train_grads, lax.all_gather(queries, 'dp', axis=1, tiled=True)[0]...]
    gather x4 -> x0, local copies, waits for them, and re-layouts: 3.73 us -> none  [the longest x2 2.59 us: local(): margin_weight = 1.0 - jax.nn.sigmoid(rewards[chosen] - rewards[rejected])]
    select_n x1 -> x0, other arithmetic: 0.97 us -> none  [local(): margin_weight = 1.0 - jax.nn.sigmoid(rewards[chosen] - rewards[rejected])]
  transfers between devices with their start and end apart: 1 -> 0, of which waited for: 1 -> 0; matrix products, arithmetic and copies ran while one was open for 11% -> 0% of each run, Pallas kernels for 0% -> 0%
where the time goes in v1:
time: 27.7 us; the launch traced here: 27.4 us
  Pallas kernels  20 us (72%)
  local copies, waits for them, and re-layouts  7.35 us (27%)
    pallas_call x1, Pallas kernels, local(): pl.pallas_call(functools.partial(kernel, outer, reps, inner), out_shape=j...  20 us
    unnamed x15, local copies, waits for them, and re-layouts  7.35 us

profile of v1, /device:TPU:0, one launch (start us, length us, event | category | flops | bytes accessed | tf_op | source)
XLA Modules:
  0.0 27.4 jit_solution(6182789717298164266)
XLA Ops:
  0.0 0.0 copy-start
  0.0 1.3 %copy-done = bf16[1,128,5120]{2,1,0:T(8,128)(2,1)S(1)} copy-done((bf16[1,128,5120]{2,1,0:T(8,128)(2,1)S(1)}, bf16[1,128,5120]{2,1,0:T(8,128)(2,1)}, u32[]{:S(2)}) %copy-start) | copy-done | bytes 1310744
  1.3 0.0 copy-start.1
  1.3 1.3 %copy-done.1 = bf16[1,128,5120]{2,1,0:T(8,128)(2,1)S(1)} copy-done((bf16[1,128,5120]{2,1,0:T(8,128)(2,1)S(1)}, bf16[1,128,5120]{2,1,0:T(8,128)(2,1)}, u32[]{:S(2)}) %copy-start.1) | copy-done | bytes 1310744
  2.6 0.0 copy-start.2
  2.6 1.3 %copy-done.2 = bf16[1,5120,128]{2,1,0:T(8,128)(2,1)S(1)} copy-done((bf16[1,5120,128]{2,1,0:T(8,128)(2,1)S(1)}, bf16[1,5120,128]{2,1,0:T(8,128)(2,1)}, u32[]{:S(2)}) %copy-start.2) | copy-done | bytes 1310744
  4.0 0.0 copy-start.3
  4.0 0.8 %copy-done.3 = bf16[1,8,4096]{2,1,0:T(8,128)(2,1)S(1)} copy-done((bf16[1,8,4096]{2,1,0:T(8,128)(2,1)S(1)}, bf16[1,8,4096]{2,1,0:T(8,128)(2,1)}, u32[]{:S(2)}) %copy-start.3) | copy-done | bytes 65560
  4.8 0.0 copy-start.4
  4.8 0.7 %copy-done.4 = s32[2,2]{1,0:T(2,128)S(1)} copy-done((s32[2,2]{1,0:T(2,128)S(1)}, s32[2,2]{1,0:T(2,128)}, u32[]{:S(2)}) %copy-start.4) | copy-done | bytes 40
  5.5 0.0 copy-start.5
  5.5 0.7 %copy-done.5 = f32[4]{0:T(128)S(1)} copy-done((f32[4]{0:T(128)S(1)}, f32[4]{0:T(128)}, u32[]{:S(2)}) %copy-start.5) | copy-done | bytes 40
  6.1 0.0 copy-start.6
  6.1 0.7 %copy-done.6 = s32[4]{0:T(128)S(1)} copy-done((s32[4]{0:T(128)S(1)}, s32[4]{0:T(128)}, u32[]{:S(2)}) %copy-start.6) | copy-done | bytes 40
  6.8 20.0 %shard_map.73 = f32[2,256]{1,0:T(2,128)S(1)} custom-call(bf16[1,128,5120]{2,1,0:T(8,128)(2,1)S(1)} %copy-done, bf16[1,128,5120]{2,1,0:T(8,128)(2,1)S(1)} %copy-done.1, bf16[1,5120,128]{2,1,0:T(8,128)(2,1)S(1)} %copy-done.2, f32[4]{0:T(128)S(1)} %copy-done.5, s32[4]{0:T(128)S(1)} %copy-done.6, s32[2,2]{1,0:T(2,128)S(1)} %copy-done.4, ...), custom_call_target="tpu_custom_call" | custom-call | tf_op jit(solution)/shard_map/pallas_call | solution.py:200
  26.8 0.6 %copy.9 = f32[2,256]{1,0:T(2,128)} copy(f32[2,256]{1,0:T(2,128)S(1)} %shard_map.73) | data formatting | bytes 4096
Async XLA Ops:
  0.0 1.3 %copy-start = (bf16[1,128,5120]{2,1,0:T(8,128)(2,1)S(1)}, bf16[1,128,5120]{2,1,0:T(8,128)(2,1)}, u32[]{:S(2)}) copy-start(bf16[1,128,5120]{2,1,0:T(8,128)(2,1)} %act_ref.1) | copy-start | bytes 3932164
  1.3 1.3 %copy-start.1 = (bf16[1,128,5120]{2,1,0:T(8,128)(2,1)S(1)}, bf16[1,128,5120]{2,1,0:T(8,128)(2,1)}, u32[]{:S(2)}) copy-start(bf16[1,128,5120]{2,1,0:T(8,128)(2,1)} %grad_ref.1) | copy-start | bytes 3932164
  2.6 1.3 %copy-start.2 = (bf16[1,5120,128]{2,1,0:T(8,128)(2,1)S(1)}, bf16[1,5120,128]{2,1,0:T(8,128)(2,1)}, u32[]{:S(2)}) copy-start(bf16[1,5120,128]{2,1,0:T(8,128)(2,1)} %proj_ref.1) | copy-start | bytes 3932164
  4.0 0.8 %copy-start.3 = (bf16[1,8,4096]{2,1,0:T(8,128)(2,1)S(1)}, bf16[1,8,4096]{2,1,0:T(8,128)(2,1)}, u32[]{:S(2)}) copy-start(bf16[1,8,4096]{2,1,0:T(8,128)(2,1)} %queries_ref.1) | copy-start | bytes 196612
  4.8 0.7 %copy-start.4 = (s32[2,2]{1,0:T(2,128)S(1)}, s32[2,2]{1,0:T(2,128)}, u32[]{:S(2)}) copy-start(s32[2,2]{1,0:T(2,128)} %pairing_ref.1) | copy-start | bytes 52
  5.5 0.7 %copy-start.5 = (f32[4]{0:T(128)S(1)}, f32[4]{0:T(128)}, u32[]{:S(2)}) copy-start(f32[4]{0:T(128)} %rewards_ref.1) | copy-start | bytes 52
  6.1 0.7 %copy-start.6 = (s32[4]{0:T(128)S(1)}, s32[4]{0:T(128)}, u32[]{:S(2)}) copy-start(s32[4]{0:T(128)} %lengths_ref.1) | copy-start | bytes 52

commit v2 on v1

--- a/solution.py
+++ b/solution.py
@@ -14,9 +14,9 @@
 
 def kernel(
     outer, reps, inner,
-    act_ref, grad_ref, proj_ref, rewards_ref, lengths_ref, pairing_ref, queries_ref, out_ref,
+    act_ref, grad_ref, proj_ref, rewards_hbm, lengths_hbm, pairing_hbm, queries_ref, out_ref,
     tokens, weights, query_all, outer_products, train_send, train_recv, part_send, part_recv,
-    load_sem, own_sem, q1_send, q1_recv, q2_send, q2_recv, t_send, t_recv, p_send, p_recv,
+    rewards_ref, lengths_ref, pairing_ref, small_sem, load_sem, own_sem, q1_send, q1_recv, q2_send, q2_recv, t_send, t_recv, p_send, p_recv,
 ):
     group = outer * inner
     me = lax.axis_index("dp")
@@ -25,10 +25,10 @@
     slab = me // (inner * reps)
     mine = slab * inner + place
     slots, width = act_ref.shape[1], act_ref.shape[2]
-    seq_count = lengths_ref.shape[0]
+    seq_count = lengths_hbm.shape[0]
     seq_len = slots // seq_count
     half = proj_ref.shape[2] // 2
-    pair_count = pairing_ref.shape[0]
+    pair_count = pairing_hbm.shape[0]
     entries = queries_ref.shape[2] // group
     rows = entries // LANES
 
@@ -60,6 +60,13 @@
 
     own = pltpu.make_async_copy(chunk_of(mine), query_all.at[slab, rep, place], own_sem)
     own.start()
+    small = [
+        pltpu.make_async_copy(rewards_hbm, rewards_ref, small_sem.at[0]),
+        pltpu.make_async_copy(lengths_hbm, lengths_ref, small_sem.at[1]),
+        pltpu.make_async_copy(pairing_hbm, pairing_ref, small_sem.at[2]),
+    ]
+    for copy in small:
+        copy.start()
 
     barrier = pltpu.get_barrier_semaphore()
     for step in range(1, group):
@@ -87,6 +94,8 @@
             chunk_of(other), query_all.at[slab, rep, place], q1_send.at[step], q1_recv.at[step], device
         ))
 
+    for copy in small:
+        copy.wait()
     lane = lax.broadcasted_iota(jnp.int32, (seq_len, LANES), 1)
     spot = lax.broadcasted_iota(jnp.int32, (seq_len, LANES), 0)
     signs = []
@@ -195,12 +204,11 @@
         entries = length // group
         rows = pair_count * entries // LANES
         dma = lambda *shape: pltpu.SemaphoreType.DMA(shape)
-        smem = pl.BlockSpec(memory_space=pltpu.SMEM)
-        hbm = pl.BlockSpec(memory_space=pl.ANY)
+        hbm = pl.BlockSpec(memory_space=pltpu.HBM)
         partial_scores = pl.pallas_call(
             functools.partial(kernel, outer, reps, inner),
             out_shape=jax.ShapeDtypeStruct((pair_count, devices * per_device), jnp.float32),
-            in_specs=[hbm, hbm, hbm, smem, smem, smem, hbm],
+            in_specs=[hbm] * 7,
             out_specs=pl.BlockSpec(memory_space=pltpu.VMEM),
             scratch_shapes=[
                 pltpu.VMEM((2 * slots, width), jnp.bfloat16),
@@ -211,11 +219,14 @@
                 pltpu.VMEM((group, rows, LANES), jnp.float32),
                 pltpu.VMEM((group, pair_count, devices * per_device), jnp.float32),
                 pltpu.VMEM((group, pair_count, devices * per_device), jnp.float32),
-                dma(CHUNKS, 3), dma(), dma(group), dma(group), dma(reps), dma(reps),
+                pltpu.SMEM(rewards.shape, rewards.dtype),
+                pltpu.SMEM(lengths.shape, lengths.dtype),
+                pltpu.SMEM(pairing.shape, pairing.dtype),
+                dma(3), dma(CHUNKS, 3), dma(), dma(group), dma(group), dma(reps), dma(reps),
                 dma(group), dma(group), dma(group), dma(group),
             ],
             compiler_params=pltpu.CompilerParams(
-                collective_id=0, has_side_effects=True, vmem_limit_bytes=40 * 1024 * 1024
+                collective_id=0, has_side_effects=True, vmem_limit_bytes=56 * 1024 * 1024
             ),
         )(activations, out_grads, projectors, rewards, lengths, pairing, queries)
         return lax.psum_scatter(partial_scores, "layer", scatter_dimension=1, tiled=True)

time: 27.7 us -> 21.1 us (0.76)
  local copies, waits for them, and re-layouts: 7.35 us -> 1.26 us
  Pallas kernels: 20 us -> 19.7 us
    unnamed x15 -> x1, local copies, waits for them, and re-layouts: 7.35 us -> 1.26 us
    pallas_call x1, Pallas kernels: 20 us -> 19.7 us  [local(): pl.pallas_call(functools.partial(kernel, outer, reps, inner), out_shape=j...]
where the time goes in v2:
time: 21.1 us; the launch traced here: 20.9 us
  Pallas kernels  19.7 us (93%)
  local copies, waits for them, and re-layouts  1.26 us (6%)
    pallas_call x1, Pallas kernels, local(): pl.pallas_call(functools.partial(kernel, outer, reps, inner), out_shape=j...  19.7 us
    unnamed x1, local copies, waits for them, and re-layouts  1.26 us

profile of v2, /device:TPU:0, one launch (start us, length us, event | category | flops | bytes accessed | tf_op | source)
XLA Modules:
  0.0 20.9 jit_solution(7693713632256661885)
XLA Ops:
  0.0 19.7 %shard_map.73 = f32[2,256]{1,0:T(2,128)} custom-call(bf16[1,128,5120]{2,1,0:T(8,128)(2,1)} %act_ref.1, bf16[1,128,5120]{2,1,0:T(8,128)(2,1)} %grad_ref.1, bf16[1,5120,128]{2,1,0:T(8,128)(2,1)} %proj_ref.1, f32[4]{0:T(128)} %rewards_hbm.1, s32[4]{0:T(128)} %lengths_hbm.1, s32[2,2]{1,0:T(2,128)} %pairing_hbm.1, bf16[1,8,4096]{2,1,0:T(8,128)(2,1)} %queries_ref.1), custom_call_target="tpu_custom_call" | custom-call | tf_op jit(solution)/shard_map/pallas_call | solution.py:208
  19.7 1.3 %copy.9 = f32[2,256]{1,0:T(2,128)} copy(f32[2,256]{1,0:T(2,128)} %shard_map.73) | data formatting | bytes 4096

commit v3 on v2

--- a/solution.py
+++ b/solution.py
@@ -33,27 +33,43 @@
     rows = entries // LANES
 
     def member(step):
-        other = (mine + step) % group
-        return other, (other // inner * reps + rep) * inner + other % inner
+        other = lax.rem(mine + step, group)
+        return other, (other // inner * reps + rep) * inner + lax.rem(other, inner)
 
     def twin(step):
-        return (slab * reps + (rep + step) % reps) * inner + place
+        return (slab * reps + lax.rem(rep + step, reps)) * inner + place
+
+    def repeat(low, high, body):
+        lax.fori_loop(low, high, lambda step, carry: (body(step), carry)[1], 0)
 
     part = width // CHUNKS
-    loads = []
-    for c in range(CHUNKS):
-        cols = pl.ds(c * part, part)
-        loads.append([
-            pltpu.make_async_copy(proj_ref.at[0, cols, :], weights.at[cols, :], load_sem.at[c, 0]),
+
+    def loads(c):
+        cols = pl.ds(pl.multiple_of(c * part, LANES), part)
+        return (
+            pltpu.make_async_copy(proj_ref.at[0, cols, :], weights.at[c], load_sem.at[c, 0]),
             pltpu.make_async_copy(
-                act_ref.at[0, :, cols], tokens.at[pl.ds(0, slots), cols], load_sem.at[c, 1]
+                act_ref.at[0, :, cols], tokens.at[c, pl.ds(0, slots), :], load_sem.at[c, 1]
             ),
             pltpu.make_async_copy(
-                grad_ref.at[0, :, cols], tokens.at[pl.ds(slots, slots), cols], load_sem.at[c, 2]
+                grad_ref.at[0, :, cols], tokens.at[c, pl.ds(slots, slots), :], load_sem.at[c, 2]
             ),
-        ])
-        for copy in loads[-1]:
+        )
+
+    def start_loads(c):
+        for copy in loads(c):
             copy.start()
+
+    barrier = pltpu.get_barrier_semaphore()
+
+    def greet(device):
+        pl.semaphore_signal(
+            barrier, inc=1, device_id={"dp": device}, device_id_type=pl.DeviceIdType.MESH
+        )
+
+    repeat(1, group, lambda step: greet(member(step)[1]))
+    repeat(1, reps, lambda step: greet(twin(step)))
+    repeat(0, CHUNKS, start_loads)
 
     def chunk_of(index):
         return queries_ref.at[0, :, pl.ds(pl.multiple_of(index * entries, LANES), entries)]
@@ -67,32 +83,21 @@
     ]
     for copy in small:
         copy.start()
-
-    barrier = pltpu.get_barrier_semaphore()
-    for step in range(1, group):
-        pl.semaphore_signal(
-            barrier, inc=1, device_id={"dp": member(step)[1]}, device_id_type=pl.DeviceIdType.MESH
-        )
-    for step in range(1, reps):
-        pl.semaphore_signal(
-            barrier, inc=1, device_id={"dp": twin(step)}, device_id_type=pl.DeviceIdType.MESH
-        )
     pl.semaphore_wait(barrier, group - 1 + reps - 1)
 
-    def send(src, dst, send_sem, recv_sem, device):
-        copy = pltpu.make_async_remote_copy(
+    def remote(src, dst, send_sem, recv_sem, device):
+        return pltpu.make_async_remote_copy(
             src_ref=src, dst_ref=dst, send_sem=send_sem, recv_sem=recv_sem,
             device_id={"dp": device}, device_id_type=pl.DeviceIdType.MESH,
         )
-        copy.start()
-        return copy
-
-    first = []
-    for step in range(1, group):
+
+    def first(step):
         other, device = member(step)
-        first.append(send(
+        return remote(
             chunk_of(other), query_all.at[slab, rep, place], q1_send.at[step], q1_recv.at[step], device
-        ))
+        )
+
+    repeat(1, group, lambda step: first(step).start())
 
     for copy in small:
         copy.wait()
@@ -115,24 +120,24 @@
             reward = rewards_ref[s]
             margin = margin + jnp.where(pairing_ref[i, 0] == s, reward, 0.0)
             margin = margin - jnp.where(pairing_ref[i, 1] == s, reward, 0.0)
-        pair_weights.append(1.0 - jax.nn.sigmoid(jnp.full((half, LANES), margin, jnp.float32)))
-
-    projected = jnp.zeros((2 * slots, 2 * half), jnp.float32)
-    for c in range(CHUNKS):
-        for copy in loads[c]:
+        pair_weights.append(1.0 - jax.nn.sigmoid(jnp.full((1, LANES), margin, jnp.float32)))
+
+    def project(c, total):
+        for copy in loads(c):
             copy.wait()
-        cols = pl.ds(c * part, part)
-        projected += jnp.dot(tokens[:, cols], weights[cols, :], preferred_element_type=jnp.float32)
+        return total + jnp.dot(tokens[c], weights[c], preferred_element_type=jnp.float32)
+
+    projected = lax.fori_loop(
+        0, CHUNKS, project, jnp.zeros((2 * slots, 2 * half), jnp.float32)
+    )
+
+    def second(step):
+        mates = query_all.at[:, rep]
+        return remote(mates, mates, q2_send.at[step], q2_recv.at[step], twin(step))
 
     own.wait()
-    for copy in first:
-        copy.wait()
-    second = [
-        send(
-            query_all.at[:, rep], query_all.at[:, rep], q2_send.at[step], q2_recv.at[step], twin(step)
-        )
-        for step in range(1, reps)
-    ]
+    repeat(1, group, lambda step: first(step).wait())
+    repeat(1, reps, lambda step: second(step).start())
 
     token_lane = lax.broadcasted_iota(jnp.int32, (slots, LANES), 1)
     act = projected[:slots]
@@ -143,7 +148,8 @@
         grad * signs, act, (((0,), (0,)), ((), ())),
         precision=lax.Precision.HIGHEST, preferred_element_type=jnp.float32,
     )
-    outer_products[...] = products * jnp.concatenate(pair_weights, axis=0)
+    for i in range(pair_count):
+        outer_products[i * half:(i + 1) * half, :] = products[i * half:(i + 1) * half] * pair_weights[i]
     lines = pair_count * half // 2
     even = outer_products[pl.ds(0, lines, stride=2), :]
     odd = outer_products[pl.ds(1, lines, stride=2), :]
@@ -153,19 +159,19 @@
         for i in range(pair_count):
             start = i * (half // 2) + g * rows
             train_send[g, i * rows:(i + 1) * rows, :] = flat[start:start + rows]
+
+    def train(step):
+        other, device = member(step)
+        return remote(
+            train_send.at[other], train_recv.at[mine], t_send.at[step], t_recv.at[step], device
+        )
+
+    repeat(1, group, lambda step: train(step).start())
     train_recv[mine] = train_send[mine]
-    train_copies = []
-    for step in range(1, group):
-        other, device = member(step)
-        train_copies.append(send(
-            train_send.at[other], train_recv.at[mine], t_send.at[step], t_recv.at[step], device
-        ))
-
-    for copy in second:
-        copy.wait()
+
+    repeat(1, reps, lambda step: second(step).wait())
     query_rows = query_all[...].astype(jnp.float32).reshape(-1, entries).astype(jnp.bfloat16)
-    for copy in train_copies:
-        copy.wait()
+    repeat(1, group, lambda step: train(step).wait())
 
     received = train_recv[...].reshape(group * pair_count, rows, LANES)
     left = jnp.concatenate([received[:, r, :] for r in range(rows)], axis=1).astype(jnp.bfloat16)
@@ -174,15 +180,16 @@
     )
     for g in range(group):
         part_send[g] = partial[g * pair_count:(g + 1) * pair_count]
+
+    def scores(step):
+        other, device = member(step)
+        return remote(
+            part_send.at[other], part_recv.at[mine], p_send.at[step], p_recv.at[step], device
+        )
+
+    repeat(1, group, lambda step: scores(step).start())
     part_recv[mine] = part_send[mine]
-    part_copies = []
-    for step in range(1, group):
-        other, device = member(step)
-        part_copies.append(send(
-            part_send.at[other], part_recv.at[mine], p_send.at[step], p_recv.at[step], device
-        ))
-    for copy in part_copies:
-        copy.wait()
+    repeat(1, group, lambda step: scores(step).wait())
     total = part_recv[0]
     for g in range(1, group):
         total += part_recv[g]
@@ -211,8 +218,8 @@
             in_specs=[hbm] * 7,
             out_specs=pl.BlockSpec(memory_space=pltpu.VMEM),
             scratch_shapes=[
-                pltpu.VMEM((2 * slots, width), jnp.bfloat16),
-                pltpu.VMEM((width, 2 * half), jnp.bfloat16),
+                pltpu.VMEM((CHUNKS, 2 * slots, width // CHUNKS), jnp.bfloat16),
+                pltpu.VMEM((CHUNKS, width // CHUNKS, 2 * half), jnp.bfloat16),
                 pltpu.VMEM((outer, reps, inner, per_device, entries), jnp.bfloat16),
                 pltpu.VMEM((pair_count * half, LANES), jnp.float32),
                 pltpu.VMEM((group, rows, LANES), jnp.float32),

time: 21.1 us -> 20.9 us (level)
  no operation moved by 1% of the time
where the time goes in v3:
time: 20.9 us; the launch traced here: 20.8 us
  Pallas kernels  19.5 us (93%)
  local copies, waits for them, and re-layouts  1.26 us (6%)
    pallas_call x1, Pallas kernels, local(): pl.pallas_call(functools.partial(kernel, outer, reps, inner), out_shape=j...  19.5 us
    unnamed x1, local copies, waits for them, and re-layouts  1.26 us

profile of v3, /device:TPU:0, one launch (start us, length us, event | category | flops | bytes accessed | tf_op | source)
XLA Modules:
  0.0 20.8 jit_solution(17463878823207501829)
XLA Ops:
  0.0 19.5 %shard_map.73 = f32[2,256]{1,0:T(2,128)} custom-call(bf16[1,128,5120]{2,1,0:T(8,128)(2,1)} %act_ref.1, bf16[1,128,5120]{2,1,0:T(8,128)(2,1)} %grad_ref.1, bf16[1,5120,128]{2,1,0:T(8,128)(2,1)} %proj_ref.1, f32[4]{0:T(128)} %rewards_hbm.1, s32[4]{0:T(128)} %lengths_hbm.1, s32[2,2]{1,0:T(2,128)} %pairing_hbm.1, bf16[1,8,4096]{2,1,0:T(8,128)(2,1)} %queries_ref.1), custom_call_target="tpu_custom_call" | custom-call | tf_op jit(solution)/shard_map/pallas_call | solution.py:215
  19.5 1.3 %copy.9 = f32[2,256]{1,0:T(2,128)} copy(f32[2,256]{1,0:T(2,128)} %shard_map.73) | data formatting | bytes 4096

commit v4 on v3

--- a/solution.py
+++ b/solution.py
@@ -198,8 +198,8 @@
 
 def solution(mesh):
     devices = mesh.shape["dp"]
-    inner = math.gcd(devices, 2)
-    outer = math.gcd(devices // inner, 4)
+    inner = 1
+    outer = math.gcd(devices, 16)
     reps = devices // (inner * outer)
     group = outer * inner
 

time: 20.9 us -> 22.6 us (1.081)
  Pallas kernels: 19.5 us -> 21.2 us
    pallas_call x1, Pallas kernels: 19.5 us -> 21.2 us  [local(): pl.pallas_call(functools.partial(kernel, outer, reps, inner), out_shape=j...]
where the time goes in v4:
time: 22.6 us; the launch traced here: 22.5 us
  Pallas kernels  21.2 us (94%)
  local copies, waits for them, and re-layouts  1.26 us (6%)
    pallas_call x1, Pallas kernels, local(): pl.pallas_call(functools.partial(kernel, outer, reps, inner), out_shape=j...  21.2 us
    unnamed x1, local copies, waits for them, and re-layouts  1.26 us

profile of v4, /device:TPU:0, one launch (start us, length us, event | category | flops | bytes accessed | tf_op | source)
XLA Modules:
  0.0 22.5 jit_solution(7338435923546267340)
XLA Ops:
  0.0 21.2 %shard_map.73 = f32[2,256]{1,0:T(2,128)} custom-call(bf16[1,128,5120]{2,1,0:T(8,128)(2,1)} %act_ref.1, bf16[1,128,5120]{2,1,0:T(8,128)(2,1)} %grad_ref.1, bf16[1,5120,128]{2,1,0:T(8,128)(2,1)} %proj_ref.1, f32[4]{0:T(128)} %rewards_hbm.1, s32[4]{0:T(128)} %lengths_hbm.1, s32[2,2]{1,0:T(2,128)} %pairing_hbm.1, bf16[1,8,4096]{2,1,0:T(8,128)(2,1)} %queries_ref.1), custom_call_target="tpu_custom_call" | custom-call | tf_op jit(solution)/shard_map/pallas_call | solution.py:215
  21.2 1.3 %copy.9 = f32[2,256]{1,0:T(2,128)} copy(f32[2,256]{1,0:T(2,128)} %shard_map.73) | data formatting | bytes 4096

commit v5 on v4

--- a/solution.py
+++ b/solution.py
@@ -16,7 +16,7 @@
     outer, reps, inner,
     act_ref, grad_ref, proj_ref, rewards_hbm, lengths_hbm, pairing_hbm, queries_ref, out_ref,
     tokens, weights, query_all, outer_products, train_send, train_recv, part_send, part_recv,
-    rewards_ref, lengths_ref, pairing_ref, small_sem, load_sem, own_sem, q1_send, q1_recv, q2_send, q2_recv, t_send, t_recv, p_send, p_recv,
+    rewards_ref, lengths_ref, pairing_ref, small_sem, load_sem, own_sem, q_send, q_recv, t_send, t_recv, p_send, p_recv,
 ):
     group = outer * inner
     me = lax.axis_index("dp")
@@ -36,8 +36,9 @@
         other = lax.rem(mine + step, group)
         return other, (other // inner * reps + rep) * inner + lax.rem(other, inner)
 
-    def twin(step):
-        return (slab * reps + lax.rem(rep + step, reps)) * inner + place
+    def stranger(step):
+        device = lax.rem(me + step, outer * reps * inner)
+        return device // (inner * reps) * inner + lax.rem(device, inner), device
 
     def repeat(low, high, body):
         lax.fori_loop(low, high, lambda step, carry: (body(step), carry)[1], 0)
@@ -67,14 +68,14 @@
             barrier, inc=1, device_id={"dp": device}, device_id_type=pl.DeviceIdType.MESH
         )
 
-    repeat(1, group, lambda step: greet(member(step)[1]))
-    repeat(1, reps, lambda step: greet(twin(step)))
+    devices = outer * reps * inner
     repeat(0, CHUNKS, start_loads)
+    repeat(1, devices, lambda step: greet(stranger(step)[1]))
 
     def chunk_of(index):
         return queries_ref.at[0, :, pl.ds(pl.multiple_of(index * entries, LANES), entries)]
 
-    own = pltpu.make_async_copy(chunk_of(mine), query_all.at[slab, rep, place], own_sem)
+    own = pltpu.make_async_copy(chunk_of(mine), query_all.at[me], own_sem)
     own.start()
     small = [
         pltpu.make_async_copy(rewards_hbm, rewards_ref, small_sem.at[0]),
@@ -83,7 +84,7 @@
     ]
     for copy in small:
         copy.start()
-    pl.semaphore_wait(barrier, group - 1 + reps - 1)
+    pl.semaphore_wait(barrier, devices - 1)
 
     def remote(src, dst, send_sem, recv_sem, device):
         return pltpu.make_async_remote_copy(
@@ -91,13 +92,13 @@
             device_id={"dp": device}, device_id_type=pl.DeviceIdType.MESH,
         )
 
-    def first(step):
-        other, device = member(step)
+    def query(step):
+        other, device = stranger(step)
         return remote(
-            chunk_of(other), query_all.at[slab, rep, place], q1_send.at[step], q1_recv.at[step], device
-        )
-
-    repeat(1, group, lambda step: first(step).start())
+            chunk_of(other), query_all.at[me], q_send.at[step], q_recv.at[step], device
+        )
+
+    repeat(1, devices, lambda step: query(step).start())
 
     for copy in small:
         copy.wait()
@@ -131,14 +132,6 @@
         0, CHUNKS, project, jnp.zeros((2 * slots, 2 * half), jnp.float32)
     )
 
-    def second(step):
-        mates = query_all.at[:, rep]
-        return remote(mates, mates, q2_send.at[step], q2_recv.at[step], twin(step))
-
-    own.wait()
-    repeat(1, group, lambda step: first(step).wait())
-    repeat(1, reps, lambda step: second(step).start())
-
     token_lane = lax.broadcasted_iota(jnp.int32, (slots, LANES), 1)
     act = projected[:slots]
     act = jnp.where(token_lane < half, act, pltpu.roll(act, half, 1))
@@ -169,7 +162,8 @@
     repeat(1, group, lambda step: train(step).start())
     train_recv[mine] = train_send[mine]
 
-    repeat(1, reps, lambda step: second(step).wait())
+    own.wait()
+    repeat(1, devices, lambda step: query(step).wait())
     query_rows = query_all[...].astype(jnp.float32).reshape(-1, entries).astype(jnp.bfloat16)
     repeat(1, group, lambda step: train(step).wait())
 
@@ -198,8 +192,8 @@
 
 def solution(mesh):
     devices = mesh.shape["dp"]
-    inner = 1
-    outer = math.gcd(devices, 16)
+    inner = math.gcd(devices, 8)
+    outer = 1
     reps = devices // (inner * outer)
     group = outer * inner
 
@@ -220,7 +214,7 @@
             scratch_shapes=[
                 pltpu.VMEM((CHUNKS, 2 * slots, width // CHUNKS), jnp.bfloat16),
                 pltpu.VMEM((CHUNKS, width // CHUNKS, 2 * half), jnp.bfloat16),
-                pltpu.VMEM((outer, reps, inner, per_device, entries), jnp.bfloat16),
+                pltpu.VMEM((devices, per_device, entries), jnp.bfloat16),
                 pltpu.VMEM((pair_count * half, LANES), jnp.float32),
                 pltpu.VMEM((group, rows, LANES), jnp.float32),
                 pltpu.VMEM((group, rows, LANES), jnp.float32),
@@ -229,7 +223,7 @@
                 pltpu.SMEM(rewards.shape, rewards.dtype),
                 pltpu.SMEM(lengths.shape, lengths.dtype),
                 pltpu.SMEM(pairing.shape, pairing.dtype),
-                dma(3), dma(CHUNKS, 3), dma(), dma(group), dma(group), dma(reps), dma(reps),
+                dma(3), dma(CHUNKS, 3), dma(), dma(devices), dma(devices),
                 dma(group), dma(group), dma(group), dma(group),
             ],
             compiler_params=pltpu.CompilerParams(

time: 22.6 us -> 20.5 us (0.907)
  Pallas kernels: 21.2 us -> 19.1 us
    pallas_call x1, Pallas kernels: 21.2 us -> 19.1 us  [local(): pl.pallas_call(functools.partial(kernel, outer, reps, inner), out_shape=j...]
where the time goes in v5:
time: 20.5 us; the launch traced here: 20.4 us
  Pallas kernels  19.1 us (93%)
  local copies, waits for them, and re-layouts  1.26 us (6%)
    pallas_call x1, Pallas kernels, local(): pl.pallas_call(functools.partial(kernel, outer, reps, inner), out_shape=j...  19.1 us
    unnamed x1, local copies, waits for them, and re-layouts  1.26 us

profile of v5, /device:TPU:0, one launch (start us, length us, event | category | flops | bytes accessed | tf_op | source)
XLA Modules:
  0.0 20.4 jit_solution(699021815019082934)
XLA Ops:
  0.0 19.1 %shard_map.73 = f32[2,256]{1,0:T(2,128)} custom-call(bf16[1,128,5120]{2,1,0:T(8,128)(2,1)} %act_ref.1, bf16[1,128,5120]{2,1,0:T(8,128)(2,1)} %grad_ref.1, bf16[1,5120,128]{2,1,0:T(8,128)(2,1)} %proj_ref.1, f32[4]{0:T(128)} %rewards_hbm.1, s32[4]{0:T(128)} %lengths_hbm.1, s32[2,2]{1,0:T(2,128)} %pairing_hbm.1, bf16[1,8,4096]{2,1,0:T(8,128)(2,1)} %queries_ref.1), custom_call_target="tpu_custom_call" | custom-call | tf_op jit(solution)/shard_map/pallas_call | solution.py:209
  19.1 1.3 %copy.9 = f32[2,256]{1,0:T(2,128)} copy(f32[2,256]{1,0:T(2,128)} %shard_map.73) | data formatting | bytes 4096

commit v6 on v5

--- a/solution.py
+++ b/solution.py
@@ -92,10 +92,14 @@
             device_id={"dp": device}, device_id_type=pl.DeviceIdType.MESH,
         )
 
+    def all_of(ref, send_sem, recv_sem):
+        blocks = ref.at[pl.ds(0, ref.shape[0] - 1)]
+        return remote(blocks, blocks, send_sem, recv_sem, stranger(1)[1])
+
     def query(step):
         other, device = stranger(step)
         return remote(
-            chunk_of(other), query_all.at[me], q_send.at[step], q_recv.at[step], device
+            chunk_of(other), query_all.at[me], q_send, q_recv, device
         )
 
     repeat(1, devices, lambda step: query(step).start())
@@ -156,16 +160,18 @@
     def train(step):
         other, device = member(step)
         return remote(
-            train_send.at[other], train_recv.at[mine], t_send.at[step], t_recv.at[step], device
+            train_send.at[other], train_recv.at[mine], t_send, t_recv, device
         )
 
     repeat(1, group, lambda step: train(step).start())
     train_recv[mine] = train_send[mine]
 
     own.wait()
-    repeat(1, devices, lambda step: query(step).wait())
+    queries_sent = all_of(query_all, q_send, q_recv)
+    queries_sent.wait_recv()
     query_rows = query_all[...].astype(jnp.float32).reshape(-1, entries).astype(jnp.bfloat16)
-    repeat(1, group, lambda step: train(step).wait())
+    train_sent = all_of(train_recv, t_send, t_recv)
+    train_sent.wait_recv()
 
     received = train_recv[...].reshape(group * pair_count, rows, LANES)
     left = jnp.concatenate([received[:, r, :] for r in range(rows)], axis=1).astype(jnp.bfloat16)
@@ -178,12 +184,16 @@
     def scores(step):
         other, device = member(step)
         return remote(
-            part_send.at[other], part_recv.at[mine], p_send.at[step], p_recv.at[step], device
+            part_send.at[other], part_recv.at[mine], p_send, p_recv, device
         )
 
     repeat(1, group, lambda step: scores(step).start())
     part_recv[mine] = part_send[mine]
-    repeat(1, group, lambda step: scores(step).wait())
+    scores_sent = all_of(part_recv, p_send, p_recv)
+    queries_sent.wait_send()
+    train_sent.wait_send()
+    scores_sent.wait_send()
+    scores_sent.wait_recv()
     total = part_recv[0]
     for g in range(1, group):
         total += part_recv[g]
@@ -204,7 +214,7 @@
         per_device, length = queries.shape[1:]
         entries = length // group
         rows = pair_count * entries // LANES
-        dma = lambda *shape: pltpu.SemaphoreType.DMA(shape)
+        dma = lambda *shape: pltpu.SemaphoreType.DMA(shape) if shape else pltpu.SemaphoreType.DMA
         hbm = pl.BlockSpec(memory_space=pltpu.HBM)
         partial_scores = pl.pallas_call(
             functools.partial(kernel, outer, reps, inner),
@@ -223,8 +233,7 @@
                 pltpu.SMEM(rewards.shape, rewards.dtype),
                 pltpu.SMEM(lengths.shape, lengths.dtype),
                 pltpu.SMEM(pairing.shape, pairing.dtype),
-                dma(3), dma(CHUNKS, 3), dma(), dma(devices), dma(devices),
-                dma(group), dma(group), dma(group), dma(group),
+                dma(3), dma(CHUNKS, 3), dma(), dma(), dma(), dma(), dma(), dma(), dma(),
             ],
             compiler_params=pltpu.CompilerParams(
                 collective_id=0, has_side_effects=True, vmem_limit_bytes=56 * 1024 * 1024

time: 20.5 us -> 19.6 us (0.956)
  Pallas kernels: 19.1 us -> 18.2 us
    pallas_call x1, Pallas kernels: 19.1 us -> 18.2 us  [local(): pl.pallas_call(functools.partial(kernel, outer, reps, inner), out_shape=j...]
where the time goes in v6:
time: 19.6 us; the launch traced here: 19.5 us
  Pallas kernels  18.2 us (93%)
  local copies, waits for them, and re-layouts  1.26 us (6%)
    pallas_call x1, Pallas kernels, local(): pl.pallas_call(functools.partial(kernel, outer, reps, inner), out_shape=j...  18.2 us
    unnamed x1, local copies, waits for them, and re-layouts  1.26 us

profile of v6, /device:TPU:0, one launch (start us, length us, event | category | flops | bytes accessed | tf_op | source)
XLA Modules:
  0.0 19.5 jit_solution(5169443009505197008)
XLA Ops:
  0.0 18.2 %shard_map.73 = f32[2,256]{1,0:T(2,128)} custom-call(bf16[1,128,5120]{2,1,0:T(8,128)(2,1)} %act_ref.1, bf16[1,128,5120]{2,1,0:T(8,128)(2,1)} %grad_ref.1, bf16[1,5120,128]{2,1,0:T(8,128)(2,1)} %proj_ref.1, f32[4]{0:T(128)} %rewards_hbm.1, s32[4]{0:T(128)} %lengths_hbm.1, s32[2,2]{1,0:T(2,128)} %pairing_hbm.1, bf16[1,8,4096]{2,1,0:T(8,128)(2,1)} %queries_ref.1), custom_call_target="tpu_custom_call" | custom-call | tf_op jit(solution)/shard_map/pallas_call | solution.py:219
  18.2 1.3 %copy.9 = f32[2,256]{1,0:T(2,128)} copy(f32[2,256]{1,0:T(2,128)} %shard_map.73) | data formatting | bytes 4096

commit v7 on v6

--- a/solution.py
+++ b/solution.py
@@ -14,8 +14,8 @@
 
 def kernel(
     outer, reps, inner,
-    act_ref, grad_ref, proj_ref, rewards_hbm, lengths_hbm, pairing_hbm, queries_ref, out_ref,
-    tokens, weights, query_all, outer_products, train_send, train_recv, part_send, part_recv,
+    act_ref, grad_ref, proj_ref, rewards_hbm, lengths_hbm, pairing_hbm, queries_ref, part_recv,
+    tokens, weights, query_all, outer_products, train_send, train_recv, part_send,
     rewards_ref, lengths_ref, pairing_ref, small_sem, load_sem, own_sem, q_send, q_recv, t_send, t_recv, p_send, p_recv,
 ):
     group = outer * inner
@@ -188,16 +188,14 @@
         )
 
     repeat(1, group, lambda step: scores(step).start())
-    part_recv[mine] = part_send[mine]
+    kept = pltpu.make_async_copy(part_send.at[mine], part_recv.at[mine], own_sem)
+    kept.start()
     scores_sent = all_of(part_recv, p_send, p_recv)
     queries_sent.wait_send()
     train_sent.wait_send()
     scores_sent.wait_send()
     scores_sent.wait_recv()
-    total = part_recv[0]
-    for g in range(1, group):
-        total += part_recv[g]
-    out_ref[...] = total
+    kept.wait()
 
 
 def solution(mesh):
@@ -218,9 +216,9 @@
         hbm = pl.BlockSpec(memory_space=pltpu.HBM)
         partial_scores = pl.pallas_call(
             functools.partial(kernel, outer, reps, inner),
-            out_shape=jax.ShapeDtypeStruct((pair_count, devices * per_device), jnp.float32),
+            out_shape=jax.ShapeDtypeStruct((group, pair_count, devices * per_device), jnp.float32),
             in_specs=[hbm] * 7,
-            out_specs=pl.BlockSpec(memory_space=pltpu.VMEM),
+            out_specs=hbm,
             scratch_shapes=[
                 pltpu.VMEM((CHUNKS, 2 * slots, width // CHUNKS), jnp.bfloat16),
                 pltpu.VMEM((CHUNKS, width // CHUNKS, 2 * half), jnp.bfloat16),
@@ -228,7 +226,6 @@
                 pltpu.VMEM((pair_count * half, LANES), jnp.float32),
                 pltpu.VMEM((group, rows, LANES), jnp.float32),
                 pltpu.VMEM((group, rows, LANES), jnp.float32),
-                pltpu.VMEM((group, pair_count, devices * per_device), jnp.float32),
                 pltpu.VMEM((group, pair_count, devices * per_device), jnp.float32),
                 pltpu.SMEM(rewards.shape, rewards.dtype),
                 pltpu.SMEM(lengths.shape, lengths.dtype),
@@ -239,7 +236,7 @@
                 collective_id=0, has_side_effects=True, vmem_limit_bytes=56 * 1024 * 1024
             ),
         )(activations, out_grads, projectors, rewards, lengths, pairing, queries)
-        return lax.psum_scatter(partial_scores, "layer", scatter_dimension=1, tiled=True)
+        return lax.psum_scatter(partial_scores.sum(axis=0), "layer", scatter_dimension=1, tiled=True)
 
     return jax.shard_map(
         local,

time: 19.6 us -> 19.3 us (0.985)
  other arithmetic: 0 us -> 1.31 us
  local copies, waits for them, and re-layouts: 1.26 us -> 0 us
  Pallas kernels: 18.2 us -> 17.7 us
    reduce_sum x0 -> x1, other arithmetic: none -> 1.31 us  [local(): partial_scores.sum(axis=0)]
    unnamed x1 -> x0, local copies, waits for them, and re-layouts: 1.26 us -> none
    pallas_call x1, Pallas kernels: 18.2 us -> 17.7 us  [local(): pl.pallas_call(functools.partial(kernel, outer, reps, inner), out_shape=j...]
where the time goes in v7:
time: 19.3 us; the launch traced here: 19 us
  Pallas kernels  17.7 us (92%)
  other arithmetic  1.31 us (7%)
    pallas_call x1, Pallas kernels, local(): pl.pallas_call(functools.partial(kernel, outer, reps, inner), out_shape=j...  17.7 us
    reduce_sum x1, other arithmetic, local(): partial_scores.sum(axis=0)  1.31 us

profile of v7, /device:TPU:0, one launch (start us, length us, event | category | flops | bytes accessed | tf_op | source)
XLA Modules:
  0.0 19.0 jit_solution(12320362182114832694)
XLA Ops:
  0.0 17.7 %shard_map.73 = f32[8,2,256]{2,1,0:T(2,128)} custom-call(bf16[1,128,5120]{2,1,0:T(8,128)(2,1)} %act_ref.1, bf16[1,128,5120]{2,1,0:T(8,128)(2,1)} %grad_ref.1, bf16[1,5120,128]{2,1,0:T(8,128)(2,1)} %proj_ref.1, f32[4]{0:T(128)} %rewards_hbm.1, s32[4]{0:T(128)} %lengths_hbm.1, s32[2,2]{1,0:T(2,128)} %pairing_hbm.1, bf16[1,8,4096]{2,1,0:T(8,128)(2,1)} %queries_ref.1), custom_call_target="tpu_custom_call" | custom-call | tf_op jit(solution)/shard_map/pallas_call | solution.py:217
  17.7 1.3 %reduce_sum.9 = f32[2,256]{1,0:T(2,128)} reduce(f32[8,2,256]{2,1,0:T(2,128)} %shard_map.73, f32[]{:T(128)} %constant.0.clone.1), dimensions={0}, to_apply=%region_0.0 | reduce | flops 3584 | bytes 18436 | tf_op jit(solution)/shard_map/reduce_sum | solution.py:239

commit v8 on v7

--- a/solution.py
+++ b/solution.py
@@ -102,7 +102,7 @@
             chunk_of(other), query_all.at[me], q_send, q_recv, device
         )
 
-    repeat(1, devices, lambda step: query(step).start())
+    repeat(0, devices - 1, lambda turn: query(lax.rem(turn + group - 1, devices - 1) + 1).start())
 
     for copy in small:
         copy.wait()

time: 19.3 us -> 19.2 us (level)
  no operation moved by 1% of the time
where the time goes in v8:
time: 19.2 us; the launch traced here: 19 us
  Pallas kernels  17.7 us (92%)
  other arithmetic  1.31 us (7%)
    pallas_call x1, Pallas kernels, local(): pl.pallas_call(functools.partial(kernel, outer, reps, inner), out_shape=j...  17.7 us
    reduce_sum x1, other arithmetic, local(): partial_scores.sum(axis=0)  1.31 us

profile of v8, /device:TPU:0, one launch (start us, length us, event | category | flops | bytes accessed | tf_op | source)
XLA Modules:
  0.0 19.0 jit_solution(11798104946582685009)
XLA Ops:
  0.0 17.7 %shard_map.73 = f32[8,2,256]{2,1,0:T(2,128)} custom-call(bf16[1,128,5120]{2,1,0:T(8,128)(2,1)} %act_ref.1, bf16[1,128,5120]{2,1,0:T(8,128)(2,1)} %grad_ref.1, bf16[1,5120,128]{2,1,0:T(8,128)(2,1)} %proj_ref.1, f32[4]{0:T(128)} %rewards_hbm.1, s32[4]{0:T(128)} %lengths_hbm.1, s32[2,2]{1,0:T(2,128)} %pairing_hbm.1, bf16[1,8,4096]{2,1,0:T(8,128)(2,1)} %queries_ref.1), custom_call_target="tpu_custom_call" | custom-call | tf_op jit(solution)/shard_map/pallas_call | solution.py:217
  17.7 1.3 %reduce_sum.9 = f32[2,256]{1,0:T(2,128)} reduce(f32[8,2,256]{2,1,0:T(2,128)} %shard_map.73, f32[]{:T(128)} %constant.0.clone.1), dimensions={0}, to_apply=%region_0.0 | reduce | flops 3584 | bytes 18436 | tf_op jit(solution)/shard_map/reduce_sum | solution.py:239
